TPU v7x, 256 devices: a whole 4x4x8 slice. The times are simulated.
256 devices in a mesh: dp: 64 (over z, y, core), outer: 4 (over x).
Axes of the slice: x: 4, y: 4, z: 8, core: 2. Of those that a mesh axis runs over, the one named last changes fastest.
Arguments:
- grad: bfloat16 [256, 524288], P(('dp', 'outer')), may hold values from -24 to 24
- momentum: float32 [256, 524288], P(('dp', 'outer')), may hold values from -6 to 6
- error: float32 [256, 524288], P(('dp', 'outer')), may hold values from -4 to 4
- variance: float32 [524288], replicated, may hold values from 0.1 to 4
- server_error: float32 [524288], P(('dp', 'outer')), may hold values from -4 to 4
Outputs:
- update: float32 [524288], replicated
- worker_error: float32 [256, 524288], P(('dp', 'outer'))
- server_residue: float32 [524288], P(('dp', 'outer'))
All inputs are finite; a program needn't handle non-finite values.
Results may differ from a plain program's by a relative error of at most 0.014.
Values may be sent and summed in bfloat16 or wider, within the bound.
A program may use at most 64 MiB of HBM per device.

v0:
```python
import jax
import jax.numpy as jnp
from jax import lax
from jax.sharding import PartitionSpec as P


def compress(values):
    blocks = values.reshape(-1, 128)
    spread = jnp.sqrt(jnp.mean(blocks * blocks, axis=1, keepdims=True) + 1e-06)
    return (spread * jnp.tanh(blocks / spread)).reshape(values.shape)


def local(grad, momentum, error, variance, server_error):
    compensated = 0.9 * momentum + 0.1 * grad.astype(jnp.float32) + error
    sent = compress(compensated).astype(jnp.bfloat16)
    worker_error = compensated - sent.astype(jnp.float32)
    owners = lax.axis_size("dp")
    groups = lax.axis_size("outer")
    length = server_error.shape[0]
    arrived = lax.all_to_all(
        sent.reshape(owners, groups * length), "dp", split_axis=0, concat_axis=0, tiled=True
    )
    partial_value = jnp.sum(arrived.astype(jnp.float32), axis=0).reshape(groups, length)
    summed = lax.psum_scatter(partial_value, "outer", scatter_dimension=0, tiled=True).reshape(
        length
    )
    average = summed / (owners * groups)
    shifted = average + server_error
    server_sent = compress(shifted).astype(jnp.bfloat16)
    server_residue = shifted - server_sent.astype(jnp.float32)
    update = lax.all_gather(server_sent, ("dp", "outer"), axis=0, tiled=True).astype(
        jnp.float32
    ) / (jnp.sqrt(variance) + 1e-08)
    return (update, worker_error, server_residue)


def solution(mesh):
    placed = (
        P(("dp", "outer"), None),
        P(("dp", "outer"), None),
        P(("dp", "outer"), None),
        P(),
        P(("dp", "outer")),
    )
    return jax.shard_map(
        local,
        mesh=mesh,
        in_specs=placed,
        out_specs=(P(), P(("dp", "outer"), None), P(("dp", "outer"))),
        check_vma=False,
    )
```

profile of v0, /device:TPU:1, one launch (start us, length us, event | category | flops | bytes accessed | tf_op | source)
XLA Modules:
  0.0 204.1 jit_solution(18015398336411412240)
XLA Ops:
  7.2 8.1 %fusion.2 = (f32[1,524288]{1,0:T(1,128)S(1)}, f32[1,524288]{1,0:T(1,128)}) fusion(f32[1,524288]{1,0:T(1,128)} %param.7, bf16[1,524288]{1,0:T(2,128)(2,1)} %param.5, f32[1,524288]{1,0:T(1,128)} %param.6), kind=kLoop, calls=%fused_computation.14 | loop fusion | flops 3145728 | bytes 9437184 | tf_op jit(solution)/shard_map/mul | solution.py:9
  15.2 0.6 reduce_sum.27
  15.8 0.0 copy-start
  15.9 0.6 mul.58
  16.5 1.0 copy-done
  17.4 5.2 %convert_subtract_fusion = (f32[1,524288]{1,0:T(1,128)}, bf16[1,524288]{1,0:T(2,128)(2,1)S(1)}) fusion(f32[1,524288]{1,0:T(1,128)S(1)} %copy-done, f32[1,524288]{1,0:T(1,128)S(1)} %bitcast.20), kind=kLoop, calls=%fused_computation | loop fusion | flops 2621440 | bytes 7340032 | tf_op jit(solution)/shard_map/sub | solution.py:16
  22.6 0.5 broadcast.39
  23.1 7.2 %reduce.1 = bf16[64,8192]{1,0:T(8,128)(2,1)S(1)} reduce(bf16[64,1,8192]{2,1,0:T(2,128)(2,1)S(1)} %bitcast.19, bf16[]{:T(256)} %broadcast.39), dimensions={1}, to_apply=%bitcast.2.reduce_sub_computation | reduce | bytes 2097154 | tf_op jit(solution)/shard_map/all_to_all | solution.py:20
  30.3 0.0 copy-start.2
  30.3 1.6 reshape.53
  31.9 13.2 %all-to-all-start = ((bf16[64,2,4096]{2,1,0:T(2,128)(2,1)}), bf16[64,2,4096]{2,1,0:T(2,128)(2,1)S(1)}, u32[]{:S(2)}, u32[]{:S(2)}) async-start(bf16[64,2,4096]{2,1,0:T(2,128)(2,1)} %reshape.53), calls=%async_computation | async-start | bytes 2097152 | tf_op jit(solution)/shard_map/all_to_all | solution.py:20
  45.1 0.2 all-gather.2.cloned.1.call-start
  45.3 0.0 copy-done.2
  45.3 0.6 dynamic-slice
  45.9 0.0 copy-start.1
  45.9 27.2 %all-to-all-done = bf16[64,2,4096]{2,1,0:T(2,128)(2,1)S(1)} async-done(((bf16[64,2,4096]{2,1,0:T(2,128)(2,1)}), bf16[64,2,4096]{2,1,0:T(2,128)(2,1)S(1)}, u32[]{:S(2)}, u32[]{:S(2)}) %all-to-all-start) | async-done | bytes 1048608 | tf_op jit(solution)/shard_map/all_to_all | solution.py:20
  73.0 1.0 reshape.54
  74.1 2.5 %convert_reduce_fusion = f32[8192]{0:T(1024)S(1)} fusion(bf16[64,1,8192]{2,1,0:T(2,128)(2,1)S(1)} %reshape.54), kind=kLoop, calls=%fused_computation.2 | loop fusion | flops 1040384 | bytes 1081344 | tf_op jit(solution)/shard_map/reduce_sum | solution.py:23
  76.6 13.3 %all-reduce = f32[4,2048]{1,0:T(4,128)S(1)} all-reduce(f32[4,2048]{1,0:T(4,128)S(1)} %reshape.51), channel_id=2, replica_groups=mesh['dp'=64,'outer'=4] {'outer'}, use_global_device_ids=true, to_apply=%region_2.0.clone | all-reduce | flops 8192 | bytes 65536
  89.9 0.7 dynamic-slice_multiply_fusion
  90.6 0.0 copy-done.1
  90.6 0.1 bitcast_reduce_fusion
  90.7 0.7 convert_subtract_fusion.1
  91.4 0.0 all-gather.2.cloned.1.call-update
  91.4 101.9 %all-gather.2.cloned.1.call-done = bf16[524288]{0:T(1024)(128)(2,1)} async-done(((bf16[2048]{0:T(1024)(128)(2,1)}), bf16[524288]{0:T(1024)(128)(2,1)}) %all-gather.2.cloned.1.call-update) | async-done | bytes 1048592 | tf_op jit(solution)/shard_map/all_gather | solution.py:31
  193.4 3.9 %add_divide_fusion = f32[524288]{0:T(1024)} fusion(f32[524288]{0:T(1024)} %param.8, bf16[524288]{0:T(1024)(128)(2,1)} %all-gather.2.cloned.1.call-done), kind=kLoop, calls=%fused_computation.1 | loop fusion | flops 1572864 | bytes 5242880 | tf_op jit(solution)/shard_map/div | solution.py:31
  (3 shorter events, 0.0 us)
Async XLA Ops:
  15.8 1.6 copy-start
  30.3 15.0 %copy-start.2 = (u32[256]{0:T(256)S(1)}, u32[256]{0:T(256)}, u32[]{:S(2)}) copy-start(u32[256]{0:T(256)} %constant.24) | copy-start | bytes 3076
  31.9 41.1 %all-to-all-start = ((bf16[64,2,4096]{2,1,0:T(2,128)(2,1)}), bf16[64,2,4096]{2,1,0:T(2,128)(2,1)S(1)}, u32[]{:S(2)}, u32[]{:S(2)}) async-start(bf16[64,2,4096]{2,1,0:T(2,128)(2,1)} %reshape.53), calls=%async_computation | async-start | bytes 2097152 | tf_op jit(solution)/shard_map/all_to_all | solution.py:20
  45.1 148.3 %all-gather.2.cloned.1.call-start = ((), (), s32[]{:S(2)}) async-start(), calls=%async_computation.1 | async-start | bytes 1052672 | tf_op jit(solution)/shard_map/all_gather | solution.py:31
  45.9 44.7 %copy-start.1 = (f32[2048]{0:T(1024)S(1)}, f32[2048]{0:T(1024)}, u32[]{:S(2)}) copy-start(f32[2048]{0:T(1024)} %param.9) | copy-start | bytes 24580
Sparse Core Ops, SparseCore 0:
  91.5 101.7 all-gather.1
where the time goes:
time: 204 us
  waiting for transfers between devices  129 us (63%)
  other arithmetic  28.9 us (14%)
  between operations  14.1 us (7%)
  starting transfers between devices  13.4 us (7%)
  blocking collectives  13.3 us (7%)
  local copies, waits for them, and re-layouts  5.31 us (3%)
    all_gather x1, waiting for transfers between devices, local(): lax.all_gather(server_sent, ('dp', 'outer'), axis=0, tiled=True)  102 us
    all_to_all x1, waiting for transfers between devices, local(): lax.all_to_all(sent.reshape(owners, groups * length), 'dp', split_axis=0,...  27.2 us
    unnamed x1, blocking collectives  13.3 us
    all_to_all x1, starting transfers between devices, local(): lax.all_to_all(sent.reshape(owners, groups * length), 'dp', split_axis=0,...  13.2 us
    mul x1, other arithmetic, compress(): spread = jnp.sqrt(jnp.mean(blocks * blocks, axis=1, keepdims=True) + 1e-06)  8.06 us
    all_to_all x1, other arithmetic, local(): lax.all_to_all(sent.reshape(owners, groups * length), 'dp', split_axis=0,...  7.15 us
    sub x1, other arithmetic, local(): worker_error = compensated - sent.astype(jnp.float32)  5.19 us
    unnamed x9, local copies, waits for them, and re-layouts  4.19 us
  transfers between devices with their start and end apart: 2, of which 2 were waited for; matrix products, arithmetic and copies ran while one was open for 0% of the time, Pallas kernels for 0%

commit v1 on v0

v1 whole, which is shorter than its diff:
```python
import functools

import jax
import jax.numpy as jnp
from jax import lax
from jax.experimental import pallas as pl
from jax.experimental.pallas import tpu as pltpu
from jax.sharding import PartitionSpec as P

MESH = pl.DeviceIdType.MESH
NX, NY, NZ = 4, 4, 8
SPAN = 16
CHUNK = 2 * NX * NY * SPAN
ROWS = NZ * CHUNK
AHEAD = 6
LAG1 = 2
LAG2 = 5
GLAG1 = 3
GLAG2 = 5


def compress(values):
    power = jnp.mean(values * values, axis=-1, keepdims=True) + 1e-6
    inverse = lax.rsqrt(power)
    return power * inverse * jnp.tanh(values * inverse)


def kernel(
    grad_hbm, momentum_hbm, error_hbm, variance_hbm, server_error_hbm,
    update, worker_error, server_residue,
    grad, momentum, error, scale, server_error, residue,
    sent, from_core, chip_sum, from_a1, a1_sum, from_z, partial_sum, gathered,
    in_sem, small_sem, server_send, server_recv,
    core_send, core_recv, a1_send, a1_recv, z_send, z_recv, a2_send, a2_recv,
    gz_send, gz_recv, ga_send, ga_recv, gc_send, gc_recv,
):
    dp = lax.axis_index("dp")
    x = lax.axis_index("outer")
    c = lax.rem(dp, 2)
    y = lax.rem(lax.div(dp, 2), NY)
    z = lax.div(dp, 2 * NY)
    a1 = x + c * (y - x)
    a2 = y + c * (x - y)

    def at(px, py, pz, pc):
        return ((pz * NY + py) * 2 + pc, px)

    def on_a1(d):
        return at(lax.rem(x + d * (1 - c), NX), lax.rem(y + d * c, NY), z, c)

    def on_a2(d):
        return at(lax.rem(x + d * c, NX), lax.rem(y + d * (1 - c), NY), z, c)

    def on_z(d):
        return at(x, y, lax.rem(z + d, NZ), c)

    sibling = at(x, y, z, 1 - c)

    def remote(src, dst, send, recv, device):
        return pltpu.make_async_remote_copy(
            src, dst, send, recv, device_id=device, device_id_type=MESH
        )

    def landed(like, sem):
        pltpu.make_async_copy(like, like, sem).wait()

    barrier = pltpu.get_barrier_semaphore()
    peers = [sibling]
    peers += [on_a1(d) for d in (1, 2, 3)]
    peers += [on_a2(d) for d in (1, 2, 3)]
    peers += [on_z(d) for d in range(1, NZ)]
    for peer in peers:
        pl.semaphore_signal(barrier, inc=1, device_id=peer, device_id_type=MESH)

    def order(k):
        odd = lax.rem(k, 2)
        return 4 + (1 - odd) * lax.div(k, 2) - odd * lax.div(k + 1, 2)

    def plane(k):
        return lax.rem(z + order(k), NZ)

    def loads(k):
        pz = plane(k)
        rows = pl.ds(pl.multiple_of(pz * CHUNK, CHUNK), CHUNK)
        flat = pl.ds(pl.multiple_of(pz * (CHUNK * 128), CHUNK * 128), CHUNK * 128)
        return [
            pltpu.make_async_copy(grad_hbm.at[:, flat], grad.at[:, flat], in_sem.at[0, k]),
            pltpu.make_async_copy(momentum_hbm.at[rows], momentum.at[rows], in_sem.at[1, k]),
            pltpu.make_async_copy(error_hbm.at[rows], error.at[rows], in_sem.at[2, k]),
        ]

    def start_loads(k, _):
        for copy in loads(k):
            copy.start()
        return 0

    lax.fori_loop(0, NZ, start_loads, 0)
    load_server = pltpu.make_async_copy(server_error_hbm, server_error.at[a2], small_sem.at[0])
    load_server.start()
    load_variance = pltpu.make_async_copy(variance_hbm, scale, small_sem.at[1])
    load_variance.start()

    def compress_chunk(k):
        for copy in loads(k):
            copy.wait()
        pz = plane(k)
        for py in range(NY):
            first = pl.multiple_of(pz * CHUNK + py * 128, 128)
            flat = pl.ds(pl.multiple_of(first * 128, 128 * 128), 128 * 128)
            rows = pl.ds(first, 128)
            slope = grad[:, flat].astype(jnp.float32).reshape(128, 128)
            compensated = 0.9 * momentum[rows, :] + 0.1 * slope + error[rows, :]
            rounded = compress(compensated).astype(jnp.bfloat16)
            worker_error[rows, :] = compensated - rounded.astype(jnp.float32)
            for px in range(NX):
                sent[0, pz, px, py] = rounded[px * SPAN : (px + 1) * SPAN]
                sent[1, pz, py, px] = rounded[(NX + px) * SPAN : (NX + px + 1) * SPAN]

    def send_core(k):
        pz = plane(k)
        remote(sent.at[1 - c, pz], from_core.at[pz], core_send, core_recv.at[k], sibling).start()

    def sum_chip(k):
        pz = plane(k)
        landed(from_core.at[pz], core_recv.at[k])
        total = sent[c, pz].astype(jnp.float32) + from_core[pz].astype(jnp.float32)
        chip_sum[pz] = total.astype(jnp.bfloat16)
        for d in (2, 1, 3):
            to = lax.rem(a1 + d, 4)
            remote(
                chip_sum.at[pz, to], from_a1.at[pz, d - 1], a1_send, a1_recv.at[k], on_a1(d)
            ).start()

    def sum_a1(k):
        pz = plane(k)
        landed(from_a1.at[pz], a1_recv.at[k])
        total = chip_sum[pz, a1].astype(jnp.float32)
        for d in range(3):
            total += from_a1[pz, d].astype(jnp.float32)
        a1_sum[pz] = total.astype(jnp.bfloat16)

        @pl.when(k < NZ - 1)
        def _():
            d = order(k)
            remote(a1_sum.at[pz], from_z.at[d - 1], z_send, z_recv.at[d - 1], on_z(d)).start()

    def compress_only(k, _):
        compress_chunk(k)
        return 0

    def send_only(k, _):
        send_core(k)
        return 0

    def step(t, _):
        @pl.when(t < NZ)
        def _():
            compress_chunk(t)
            send_core(t)

        @pl.when(jnp.logical_and(t >= LAG1, t < NZ + LAG1))
        def _():
            sum_chip(t - LAG1)

        @pl.when(t >= LAG2)
        def _():
            sum_a1(t - LAG2)

        return 0

    lax.fori_loop(0, AHEAD, compress_only, 0)
    pl.semaphore_wait(barrier, len(peers))
    lax.fori_loop(0, AHEAD, send_only, 0)
    load_server.wait()
    for d in (2, 1, 3):
        remote(
            server_error.at[a2], server_error.at[a2], server_send, server_recv.at[d - 1], on_a2(d)
        ).start()

    def early(t, _):
        sum_chip(t)
        return 0

    if AHEAD > LAG1:
        lax.fori_loop(0, AHEAD - LAG1, early, 0)
    early_a1 = max(AHEAD - LAG2, 0)
    for k in range(early_a1):
        sum_a1(jnp.int32(k))
    lax.fori_loop(AHEAD, NZ + LAG2, step, 0)

    total = a1_sum[z].astype(jnp.float32)
    for d in range(NZ - 1):
        landed(from_z.at[d], z_recv.at[d])
        total += from_z[d].astype(jnp.float32)
    partial_sum[a2] = total.astype(jnp.bfloat16)
    for d in (2, 1, 3):
        remote(
            partial_sum.at[a2], partial_sum.at[a2], a2_send, a2_recv.at[d - 1], on_a2(d)
        ).start()

    load_variance.wait()

    def invert(i, _):
        rows = pl.ds(pl.multiple_of(i * 128, 128), 128)
        scale[rows, :] = 1.0 / (jnp.sqrt(scale[rows, :]) + 1e-8)
        return 0

    lax.fori_loop(0, ROWS // 128, invert, 0)

    for d in (1, 2, 3):
        landed(server_error.at[0], server_recv.at[d - 1])
    for d in (1, 2, 3):
        landed(partial_sum.at[0], a2_recv.at[d - 1])
    summed = partial_sum[0].astype(jnp.float32)
    for j in range(1, 4):
        summed += partial_sum[j].astype(jnp.float32)
    shifted = summed * (1.0 / (2 * NX * NY * NZ)) + server_error[...]
    answer = compress(shifted).astype(jnp.bfloat16)
    gathered[c, z, a1] = answer
    residue[...] = shifted - answer.astype(jnp.float32)

    mine = gathered.at[c, z, a1]
    for d in (4, 3, 5, 2, 6, 1, 7):
        remote(mine, mine, gz_send, gz_recv.at[d - 1], on_z(d)).start()
    server_residue[...] = residue[a2]

    def source(k):
        odd = lax.rem(k, 2)
        away = odd * lax.div(k + 1, 2) - (1 - odd) * lax.div(k, 2)
        return lax.rem(z + away + NZ, NZ)

    def forward_a1(k):
        pz = source(k)

        @pl.when(k > 0)
        def _():
            landed(gathered.at[c, pz, a1], gz_recv.at[lax.rem(z - pz + NZ, NZ) - 1])

        block = gathered.at[c, pz, a1]
        for d in (2, 1, 3):
            remote(block, block, ga_send, ga_recv.at[k], on_a1(d)).start()

    def finish(pz, pc):
        for py in range(NY):
            for px in range(NX):
                i1 = px + pc * (py - px)
                i2 = py + pc * (px - py)
                first = pz * CHUNK + py * 128 + pc * 64 + px * SPAN
                rows = pl.ds(pl.multiple_of(first, SPAN), SPAN)
                update[rows, :] = gathered[pc, pz, i1, i2].astype(jnp.float32) * scale[rows, :]

    def forward_core(k):
        pz = source(k)
        landed(from_a1.at[pz], ga_recv.at[k])
        block = gathered.at[c, pz]
        remote(block, block, gc_send, gc_recv.at[k], sibling).start()
        finish(pz, c)

    def last(k):
        pz = source(k)
        landed(gathered.at[1 - c, pz], gc_recv.at[k])
        finish(pz, 1 - c)

    def gather(t, _):
        @pl.when(t < NZ)
        def _():
            forward_a1(t)

        @pl.when(jnp.logical_and(t >= GLAG1, t < NZ + GLAG1))
        def _():
            forward_core(t - GLAG1)

        @pl.when(t >= GLAG2)
        def _():
            last(t - GLAG2)

        return 0

    lax.fori_loop(0, NZ + GLAG2, gather, 0)

    landed(from_core, core_send)
    landed(from_a1, a1_send)
    landed(from_z, z_send)
    landed(partial_sum.at[pl.ds(0, 3)], a2_send)
    landed(server_error.at[pl.ds(0, 3)], server_send)
    landed(from_z, gz_send)
    landed(from_a1, ga_send)
    landed(from_core, gc_send)


def local(grad, momentum, error, variance, server_error):
    f32, bf16, dma = jnp.float32, jnp.bfloat16, pltpu.SemaphoreType.DMA
    whole = (ROWS, 128)
    update, worker_error, server_residue = pl.pallas_call(
        kernel,
        name="exchange",
        out_shape=(
            pltpu.VMEM(whole, f32),
            pltpu.VMEM(whole, f32),
            pltpu.VMEM((SPAN, 128), f32),
        ),
        in_specs=[pl.BlockSpec(memory_space=pltpu.HBM)] * 5,
        out_specs=[pl.BlockSpec(memory_space=pltpu.VMEM)] * 3,
        scratch_shapes=[
            pltpu.VMEM((1, ROWS * 128), bf16),
            pltpu.VMEM(whole, f32),
            pltpu.VMEM(whole, f32),
            pltpu.VMEM(whole, f32),
            pltpu.VMEM((4, SPAN, 128), f32),
            pltpu.VMEM((4, SPAN, 128), f32),
            pltpu.VMEM((2, NZ, 4, 4, SPAN, 128), bf16),
            pltpu.VMEM((NZ, 4, 4, SPAN, 128), bf16),
            pltpu.VMEM((NZ, 4, 4, SPAN, 128), bf16),
            pltpu.VMEM((NZ, 3, 4, SPAN, 128), bf16),
            pltpu.VMEM((NZ, 4, SPAN, 128), bf16),
            pltpu.VMEM((NZ - 1, 4, SPAN, 128), bf16),
            pltpu.VMEM((4, 4, SPAN, 128), bf16),
            pltpu.VMEM((2, NZ, 4, 4, SPAN, 128), bf16),
            dma((3, NZ)),
            dma((2,)),
            dma, dma((3,)),
            dma, dma((NZ,)),
            dma, dma((NZ,)),
            dma, dma((NZ - 1,)),
            dma, dma((3,)),
            dma, dma((NZ - 1,)),
            dma, dma((NZ,)),
            dma, dma((NZ,)),
        ],
        compiler_params=pltpu.CompilerParams(
            collective_id=0, has_side_effects=True, vmem_limit_bytes=32 << 20
        ),
    )(
        *(
            pltpu.with_memory_space_constraint(operand, pltpu.HBM)
            for operand in (
                grad,
                momentum.reshape(whole),
                error.reshape(whole),
                variance.reshape(whole),
                server_error.reshape(SPAN, 128),
            )
        )
    )
    return (
        update.reshape(ROWS * 128),
        worker_error.reshape(1, ROWS * 128),
        server_residue.reshape(SPAN * 128),
    )


def solution(mesh):
    placed = (
        P(("dp", "outer"), None),
        P(("dp", "outer"), None),
        P(("dp", "outer"), None),
        P(),
        P(("dp", "outer")),
    )
    return jax.shard_map(
        local,
        mesh=mesh,
        in_specs=placed,
        out_specs=(P(), P(("dp", "outer"), None), P(("dp", "outer"))),
        check_vma=False,
    )
```

time: 204 us -> 44.5 us (0.22)
  waiting for transfers between devices: 129 us -> 0 us
  Pallas kernels: 0 us -> 40.5 us
  other arithmetic: 28.9 us -> 0 us
  between operations: 14.1 us -> 0.64 us
  starting transfers between devices: 13.4 us -> 0 us
  blocking collectives: 13.3 us -> 0 us
    all_gather x1 -> x0, waiting for transfers between devices: 102 us -> none  [local(): lax.all_gather(server_sent, ('dp', 'outer'), axis=0, tiled=True)]
    pallas_call x0 -> x1, Pallas kernels: none -> 40.5 us  [local(): pl.pallas_call(kernel, name='exchange', out_shape=(pltpu.VMEM(whole, f32)...]
    all_to_all x1 -> x0, waiting for transfers between devices: 27.2 us -> none  [local(): lax.all_to_all(sent.reshape(owners, groups * length), 'dp', split_axis=0,...]
    unnamed x1 -> x0, blocking collectives: 13.3 us -> none
    all_to_all x1 -> x0, starting transfers between devices: 13.2 us -> none  [local(): lax.all_to_all(sent.reshape(owners, groups * length), 'dp', split_axis=0,...]
    mul x1 -> x0, other arithmetic: 8.06 us -> none  [compress(): spread = jnp.sqrt(jnp.mean(blocks * blocks, axis=1, keepdims=True) + 1e-06)]
    all_to_all x1 -> x0, other arithmetic: 7.15 us -> none  [local(): lax.all_to_all(sent.reshape(owners, groups * length), 'dp', split_axis=0,...]
    sub x2 -> x0, other arithmetic: 5.89 us -> none  [the longest x1 5.19 us: local(): worker_error = compensated - sent.astype(jnp.float32)]
  transfers between devices with their start and end apart: 2 -> 0, of which waited for: 2 -> 0; matrix products, arithmetic and copies ran while one was open for 0% -> 0% of each run, Pallas kernels for 0% -> 0%
where the time goes in v1:
time: 44.5 us
  Pallas kernels  40.5 us (91%)
  local copies, waits for them, and re-layouts  3.37 us (8%)
  between operations  0.64 us (1%)
    pallas_call x1, Pallas kernels, local(): pl.pallas_call(kernel, name='exchange', out_shape=(pltpu.VMEM(whole, f32)...  40.5 us
    unnamed x3, local copies, waits for them, and re-layouts  3.37 us

profile of v1, /device:TPU:1, one launch (start us, length us, event | category | flops | bytes accessed | tf_op | source)
XLA Modules:
  0.0 44.5 jit_solution(5296038354144343956)
XLA Ops:
  0.6 40.5 %exchange.1 = (f32[4096,128]{1,0:T(8,128)S(1)}, f32[4096,128]{1,0:T(8,128)S(1)}, f32[16,128]{1,0:T(8,128)S(1)}) custom-call(bf16[1,524288]{1,0:T(2,128)(2,1)} %grad_hbm.1, f32[4096,128]{1,0:T(8,128)} %bitcast.10, f32[4096,128]{1,0:T(8,128)} %bitcast.11, f32[4096,128]{1,0:T(8,128)} %bitcast.12, f32[16,128]{1,0:T(8,128)} %bitcast.13), custom_call_target="tpu_custom_call" | custom-call | tf_op jit(solution)/shard_map/exchange/pallas_call | solution.py:294
  41.1 1.5 %copy.11 = f32[524288]{0:T(1024)} copy(f32[524288]{0:T(1024)S(1)} %bitcast.8) | data formatting | bytes 4194304
  42.5 1.3 %copy.12 = f32[1,524288]{1,0:T(1,128)} copy(f32[1,524288]{1,0:T(1,128)S(1)} %bitcast.7) | data formatting | bytes 4194304
  43.9 0.6 %copy.13 = f32[2048]{0:T(1024)} copy(f32[2048]{0:T(1024)S(1)} %bitcast.9) | data formatting | bytes 16384

commit v2 on v0

v2 whole, which is shorter than its diff:
```python
import jax
import jax.numpy as jnp
from jax import lax
from jax.experimental import pallas as pl
from jax.experimental.pallas import tpu as pltpu
from jax.sharding import PartitionSpec as P

MESH = pl.DeviceIdType.MESH
NX, NY, NZ = 4, 4, 8
PLANE = NX * NY
SPAN = 16
CHUNK = 2 * PLANE * SPAN
ROWS = NZ * CHUNK
AHEAD = 1
LAG = 4
GLAG = 2
PARTS = 4

AWAY = sorted(
    ((dx, dy) for dx in range(NX) for dy in range(NY) if dx or dy),
    key=lambda d: -min(d[0], NX - d[0]) - min(d[1], NY - d[1]),
)
ABOVE = sorted(range(1, NZ), key=lambda d: -min(d, NZ - d))


def compress(values):
    power = jnp.mean(values * values, axis=-1, keepdims=True) + 1e-6
    inverse = lax.rsqrt(power)
    return power * inverse * jnp.tanh(values * inverse)


def kernel(
    grad_hbm, momentum_hbm, error_hbm, variance_hbm, server_error_hbm,
    update, worker_error, server_residue,
    grad, momentum, error, scale, server_error,
    sent, from_core, chip_sum, from_plane, plane_sum, gathered,
    in_sem, small_sem, server_send, server_recv,
    core_send, core_recv, plane_send, plane_recv, z_send, z_recv,
    gather_send, gather_recv, last_send, last_recv,
):
    dp = lax.axis_index("dp")
    x = lax.axis_index("outer")
    c = lax.rem(dp, 2)
    y = lax.rem(lax.div(dp, 2), NY)
    z = lax.div(dp, 2 * NY)

    def at(px, py, pz, pc):
        return ((pz * NY + py) * 2 + pc, px)

    sibling = at(x, y, z, 1 - c)
    plane = [(lax.rem(x + dx, NX), lax.rem(y + dy, NY)) for dx, dy in AWAY]
    column = [at(x, y, lax.rem(z + d, NZ), c) for d in ABOVE]
    me = y * NX + x

    def remote(src, dst, send, recv, device):
        return pltpu.make_async_remote_copy(
            src, dst, send, recv, device_id=device, device_id_type=MESH
        )

    def landed(like, sem):
        pltpu.make_async_copy(like, like, sem).wait()

    def each(count, body):
        def step(k, _):
            body(k)
            return 0

        lax.fori_loop(0, count, step, 0)

    def loads(k):
        rows = pl.ds(pl.multiple_of(k * CHUNK, CHUNK), CHUNK)
        flat = pl.ds(pl.multiple_of(k * (CHUNK * 128), CHUNK * 128), CHUNK * 128)
        return [
            pltpu.make_async_copy(grad_hbm.at[:, flat], grad.at[:, flat], in_sem.at[0, k]),
            pltpu.make_async_copy(momentum_hbm.at[rows], momentum.at[rows], in_sem.at[1, k]),
            pltpu.make_async_copy(error_hbm.at[rows], error.at[rows], in_sem.at[2, k]),
        ]

    def start_loads(k):
        for copy in loads(k):
            copy.start()

    each(NZ, start_loads)
    load_server = pltpu.make_async_copy(server_error_hbm, server_error.at[z], small_sem.at[0])
    load_server.start()
    load_variance = pltpu.make_async_copy(variance_hbm, scale, small_sem.at[1])
    load_variance.start()

    barrier = pltpu.get_barrier_semaphore()
    peers = [sibling] + [at(px, py, z, c) for px, py in plane] + column
    for peer in peers:
        pl.semaphore_signal(barrier, inc=1, device_id=peer, device_id_type=MESH)

    def compress_chunk(k):
        for copy in loads(k):
            copy.wait()
        for py in range(NY):
            first = pl.multiple_of(k * CHUNK + py * 128, 128)
            flat = pl.ds(pl.multiple_of(first * 128, 128 * 128), 128 * 128)
            rows = pl.ds(first, 128)
            slope = grad[:, flat].astype(jnp.float32).reshape(128, 128)
            compensated = 0.9 * momentum[rows, :] + 0.1 * slope + error[rows, :]
            rounded = compress(compensated).astype(jnp.bfloat16)
            worker_error[rows, :] = compensated - rounded.astype(jnp.float32)
            for pc in range(2):
                for px in range(NX):
                    first = (pc * NX + px) * SPAN
                    sent[pc, k, py * NX + px] = rounded[first : first + SPAN]

    def send_core(k):
        remote(sent.at[1 - c, k], from_core.at[k], core_send, core_recv.at[k], sibling).start()

    def sum_chip(k):
        landed(from_core.at[k], core_recv.at[k])
        total = sent[c, k].astype(jnp.float32) + from_core[k].astype(jnp.float32)
        chip_sum[k] = total.astype(jnp.bfloat16)
        for px, py in plane:
            remote(
                chip_sum.at[k, py * NX + px],
                from_plane.at[k, me],
                plane_send,
                plane_recv.at[k],
                at(px, py, z, c),
            ).start()
        from_plane[k, me] = chip_sum[k, me]

    def sum_plane(k):
        landed(from_plane.at[k, pl.ds(0, PLANE - 1)], plane_recv.at[k])
        total = jnp.sum(from_plane[k].astype(jnp.float32), axis=0)
        plane_sum[k, z] = total.astype(jnp.bfloat16)
        block = plane_sum.at[k, z]
        for peer in column:
            remote(block, block, z_send, z_recv.at[k], peer).start()

    def serve(k):
        landed(plane_sum.at[k, pl.ds(0, NZ - 1)], z_recv.at[k])
        total = jnp.sum(plane_sum[k].astype(jnp.float32), axis=0)
        shifted = total * (1.0 / (2 * PLANE * NZ)) + server_error[k]
        answer = compress(shifted).astype(jnp.bfloat16)
        gathered[c, k, me] = answer
        block = gathered.at[c, k, me]
        for px, py in plane:
            remote(block, block, gather_send, gather_recv.at[k], at(px, py, z, c)).start()

        @pl.when(k == z)
        def _():
            server_residue[...] = shifted - answer.astype(jnp.float32)

    def finish(k, pc):
        for py in range(NY):
            first = pl.multiple_of(k * CHUNK + py * 128 + pc * 64, 64)
            rows = pl.ds(first, 64)
            values = gathered[pc, k, py * NX : (py + 1) * NX].astype(jnp.float32)
            update[rows, :] = values.reshape(64, 128) * scale[rows, :]

    def hand_over(k):
        landed(from_plane.at[k, pl.ds(0, PLANE - 1)], gather_recv.at[k])
        block = gathered.at[c, k]
        remote(block, block, last_send, last_recv.at[k], sibling).start()
        finish(k, c)

    def take_over(k):
        landed(gathered.at[1 - c, k], last_recv.at[k])
        finish(k, 1 - c)

    each(AHEAD, compress_chunk)
    pl.semaphore_wait(barrier, len(peers))
    each(AHEAD, send_core)

    def early(t, _):
        @pl.when(t < NZ)
        def _():
            compress_chunk(t)
            send_core(t)

        @pl.when(t >= LAG)
        def _():
            sum_chip(t - LAG)

        return 0

    lax.fori_loop(AHEAD, NZ + LAG, early, 0)

    load_server.wait()
    for peer in column:
        remote(server_error.at[z], server_error.at[z], server_send, server_recv, peer).start()

    load_variance.wait()

    def invert(i):
        rows = pl.ds(pl.multiple_of(i * 128, 128), 128)
        scale[rows, :] = 1.0 / (jnp.sqrt(scale[rows, :]) + 1e-8)

    each(ROWS // 128, invert)
    each(NZ, sum_plane)
    landed(server_error.at[pl.ds(0, NZ - 1)], server_recv)
    each(NZ, serve)

    def late(t, _):
        @pl.when(t < NZ)
        def _():
            hand_over(t)

        @pl.when(t >= GLAG)
        def _():
            take_over(t - GLAG)

        return 0

    lax.fori_loop(0, NZ + GLAG, late, 0)

    landed(from_core, core_send)
    landed(from_plane.at[:, pl.ds(0, PLANE - 1)], plane_send)
    landed(plane_sum.at[:, pl.ds(0, NZ - 1)], z_send)
    landed(server_error.at[pl.ds(0, NZ - 1)], server_send)
    landed(from_plane.at[:, pl.ds(0, PLANE - 1)], gather_send)
    landed(from_core, last_send)


def store(update, worker_error, server_residue, *refs):
    outs, sem = refs[:3], refs[3]
    copies = []
    for i, (src, dst) in enumerate(zip((update, worker_error, server_residue), outs)):
        parts = PARTS if src.shape[0] == ROWS else 1
        rows = src.shape[0] // parts
        for j in range(parts):
            piece = pl.ds(j * rows, rows)
            copies.append(pltpu.make_async_copy(src.at[piece], dst.at[piece], sem.at[i, j]))
    for copy in copies:
        copy.start()
    for copy in copies:
        copy.wait()


def local(grad, momentum, error, variance, server_error):
    f32, bf16, dma = jnp.float32, jnp.bfloat16, pltpu.SemaphoreType.DMA
    whole = (ROWS, 128)
    held = pl.pallas_call(
        kernel,
        name="exchange",
        out_shape=(
            pltpu.VMEM(whole, f32),
            pltpu.VMEM(whole, f32),
            pltpu.VMEM((SPAN, 128), f32),
        ),
        in_specs=[pl.BlockSpec(memory_space=pltpu.HBM)] * 5,
        out_specs=[pl.BlockSpec(memory_space=pltpu.VMEM)] * 3,
        scratch_shapes=[
            pltpu.VMEM((1, ROWS * 128), bf16),
            pltpu.VMEM(whole, f32),
            pltpu.VMEM(whole, f32),
            pltpu.VMEM(whole, f32),
            pltpu.VMEM((NZ, SPAN, 128), f32),
            pltpu.VMEM((2, NZ, PLANE, SPAN, 128), bf16),
            pltpu.VMEM((NZ, PLANE, SPAN, 128), bf16),
            pltpu.VMEM((NZ, PLANE, SPAN, 128), bf16),
            pltpu.VMEM((NZ, PLANE, SPAN, 128), bf16),
            pltpu.VMEM((NZ, NZ, SPAN, 128), bf16),
            pltpu.VMEM((2, NZ, PLANE, SPAN, 128), bf16),
            dma((3, NZ)),
            dma((2,)),
            dma, dma,
            dma, dma((NZ,)),
            dma, dma((NZ,)),
            dma, dma((NZ,)),
            dma, dma((NZ,)),
            dma, dma((NZ,)),
        ],
        compiler_params=pltpu.CompilerParams(
            collective_id=0, has_side_effects=True, vmem_limit_bytes=32 << 20
        ),
    )(
        *(
            pltpu.with_memory_space_constraint(operand, pltpu.HBM)
            for operand in (
                grad,
                momentum.reshape(whole),
                error.reshape(whole),
                variance.reshape(whole),
                server_error.reshape(SPAN, 128),
            )
        )
    )
    update, worker_error, server_residue = pl.pallas_call(
        store,
        name="store",
        out_shape=tuple(jax.ShapeDtypeStruct(v.shape, v.dtype) for v in held),
        in_specs=[pl.BlockSpec(memory_space=pltpu.VMEM)] * 3,
        out_specs=[pl.BlockSpec(memory_space=pl.ANY)] * 3,
        scratch_shapes=[dma((3, PARTS))],
        compiler_params=pltpu.CompilerParams(vmem_limit_bytes=1 << 20),
    )(*(pltpu.with_memory_space_constraint(v, pltpu.VMEM) for v in held))
    return (
        update.reshape(ROWS * 128),
        worker_error.reshape(1, ROWS * 128),
        server_residue.reshape(SPAN * 128),
    )


def solution(mesh):
    placed = (
        P(("dp", "outer"), None),
        P(("dp", "outer"), None),
        P(("dp", "outer"), None),
        P(),
        P(("dp", "outer")),
    )
    return jax.shard_map(
        local,
        mesh=mesh,
        in_specs=placed,
        out_specs=(P(), P(("dp", "outer"), None), P(("dp", "outer"))),
        check_vma=False,
    )
```

time: 204 us -> 35.5 us (0.17)
  waiting for transfers between devices: 129 us -> 0 us
  Pallas kernels: 0 us -> 34.8 us
  other arithmetic: 28.9 us -> 0 us
  between operations: 14.1 us -> 0.64 us
  starting transfers between devices: 13.4 us -> 0 us
  blocking collectives: 13.3 us -> 0 us
  local copies, waits for them, and re-layouts: 5.31 us -> 0 us
    all_gather x1 -> x0, waiting for transfers between devices: 102 us -> none  [local(): lax.all_gather(server_sent, ('dp', 'outer'), axis=0, tiled=True)]
    pallas_call x0 -> x2, Pallas kernels: none -> 34.8 us  [the longest x1 32.7 us: local(): pl.pallas_call(kernel, name='exchange', out_shape=(pltpu.VMEM(whole, f32)...]
    all_to_all x1 -> x0, waiting for transfers between devices: 27.2 us -> none  [local(): lax.all_to_all(sent.reshape(owners, groups * length), 'dp', split_axis=0,...]
    unnamed x1 -> x0, blocking collectives: 13.3 us -> none
    all_to_all x1 -> x0, starting transfers between devices: 13.2 us -> none  [local(): lax.all_to_all(sent.reshape(owners, groups * length), 'dp', split_axis=0,...]
    mul x1 -> x0, other arithmetic: 8.06 us -> none  [compress(): spread = jnp.sqrt(jnp.mean(blocks * blocks, axis=1, keepdims=True) + 1e-06)]
    all_to_all x1 -> x0, other arithmetic: 7.15 us -> none  [local(): lax.all_to_all(sent.reshape(owners, groups * length), 'dp', split_axis=0,...]
    sub x2 -> x0, other arithmetic: 5.89 us -> none  [the longest x1 5.19 us: local(): worker_error = compensated - sent.astype(jnp.float32)]
  transfers between devices with their start and end apart: 2 -> 0, of which waited for: 2 -> 0; matrix products, arithmetic and copies ran while one was open for 0% -> 0% of each run, Pallas kernels for 0% -> 0%
where the time goes in v2:
time: 35.5 us; the launch traced here: 35.4 us
  Pallas kernels  34.8 us (98%)
  between operations  0.64 us (2%)
    pallas_call x1, Pallas kernels, local(): pl.pallas_call(kernel, name='exchange', out_shape=(pltpu.VMEM(whole, f32)...  32.7 us
    pallas_call x1, Pallas kernels, local(): pl.pallas_call(store, name='store', out_shape=tuple((jax.ShapeDtypeStruct...  2.11 us

profile of v2, /device:TPU:1, one launch (start us, length us, event | category | flops | bytes accessed | tf_op | source)
XLA Modules:
  0.0 35.4 jit_solution(11697218885375569458)
XLA Ops:
  0.6 32.7 %exchange.1 = (f32[4096,128]{1,0:T(8,128)S(1)}, f32[4096,128]{1,0:T(8,128)S(1)}, f32[16,128]{1,0:T(8,128)S(1)}) custom-call(bf16[1,524288]{1,0:T(2,128)(2,1)} %grad_hbm.1, f32[4096,128]{1,0:T(8,128)} %bitcast.7, f32[4096,128]{1,0:T(8,128)} %bitcast.8, f32[4096,128]{1,0:T(8,128)} %bitcast.9, f32[16,128]{1,0:T(8,128)} %bitcast.10), custom_call_target="tpu_custom_call" | custom-call | tf_op jit(solution)/shard_map/exchange/pallas_call | solution.py:238
  33.3 2.1 %store.1 = (f32[4096,128]{1,0:T(8,128)}, f32[4096,128]{1,0:T(8,128)}, f32[16,128]{1,0:T(8,128)}) custom-call(f32[4096,128]{1,0:T(8,128)S(1)} %get-tuple-element.9.update, f32[4096,128]{1,0:T(8,128)S(1)} %get-tuple-element.10.worker_error, f32[16,128]{1,0:T(8,128)S(1)} %get-tuple-element.11.server_residue), custom_call_target="tpu_custom_call" | custom-call | tf_op jit(solution)/shard_map/store/pallas_call | solution.py:284

commit v3 on v2

--- a/solution.py
+++ b/solution.py
@@ -11,10 +11,10 @@
 SPAN = 16
 CHUNK = 2 * PLANE * SPAN
 ROWS = NZ * CHUNK
-AHEAD = 1
-LAG = 4
-GLAG = 2
-PARTS = 4
+GREET, MEET = 2, 4
+BEFORE, READY = 6, 2
+SPREAD, SERVE, SCATTER, HAND, TAKE = 0, 7, 7, 14, 16
+PARTS = 1
 
 AWAY = sorted(
     ((dx, dy) for dx in range(NX) for dy in range(NY) if dx or dy),
@@ -32,11 +32,11 @@
 def kernel(
     grad_hbm, momentum_hbm, error_hbm, variance_hbm, server_error_hbm,
     update, worker_error, server_residue,
-    grad, momentum, error, scale, server_error,
+    grad, momentum, error, scale, server_error, residue,
     sent, from_core, chip_sum, from_plane, plane_sum, gathered,
     in_sem, small_sem, server_send, server_recv,
     core_send, core_recv, plane_send, plane_recv, z_send, z_recv,
-    gather_send, gather_recv, last_send, last_recv,
+    gather_send, last_send, word,
 ):
     dp = lax.axis_index("dp")
     x = lax.axis_index("outer")
@@ -44,13 +44,16 @@
     y = lax.rem(lax.div(dp, 2), NY)
     z = lax.div(dp, 2 * NY)
 
+    me = y * NX + x
+
     def at(px, py, pz, pc):
         return ((pz * NY + py) * 2 + pc, px)
 
     sibling = at(x, y, z, 1 - c)
     plane = [(lax.rem(x + dx, NX), lax.rem(y + dy, NY)) for dx, dy in AWAY]
-    column = [at(x, y, lax.rem(z + d, NZ), c) for d in ABOVE]
-    me = y * NX + x
+    column = [lax.rem(z + d, NZ) for d in ABOVE]
+
+    gather_recv, last_recv = in_sem.at[0], in_sem.at[1]
 
     def remote(src, dst, send, recv, device):
         return pltpu.make_async_remote_copy(
@@ -60,40 +63,46 @@
     def landed(like, sem):
         pltpu.make_async_copy(like, like, sem).wait()
 
-    def each(count, body):
+    def each(first, end, body):
         def step(k, _):
             body(k)
             return 0
 
-        lax.fori_loop(0, count, step, 0)
-
-    def loads(k):
+        lax.fori_loop(first, end, step, 0)
+
+    def load_grad(k):
+        flat = pl.ds(pl.multiple_of(k * (CHUNK * 128), CHUNK * 128), CHUNK * 128)
+        return pltpu.make_async_copy(grad_hbm.at[:, flat], grad.at[:, flat], in_sem.at[0, k])
+
+    def start_loads(k):
+        load_grad(k).start()
         rows = pl.ds(pl.multiple_of(k * CHUNK, CHUNK), CHUNK)
-        flat = pl.ds(pl.multiple_of(k * (CHUNK * 128), CHUNK * 128), CHUNK * 128)
-        return [
-            pltpu.make_async_copy(grad_hbm.at[:, flat], grad.at[:, flat], in_sem.at[0, k]),
-            pltpu.make_async_copy(momentum_hbm.at[rows], momentum.at[rows], in_sem.at[1, k]),
-            pltpu.make_async_copy(error_hbm.at[rows], error.at[rows], in_sem.at[2, k]),
-        ]
-
-    def start_loads(k):
-        for copy in loads(k):
-            copy.start()
-
-    each(NZ, start_loads)
+        for src, dst in ((momentum_hbm, momentum), (error_hbm, error)):
+            pltpu.make_async_copy(src.at[rows], dst.at[rows], in_sem.at[1, k]).start()
+
+    start_loads(0)
+    barrier = pltpu.get_barrier_semaphore()
+    others = [(px, py, z) for px, py in plane] + [(x, y, pz) for pz in column]
+
+    def signal(semaphore, device):
+        pl.semaphore_signal(semaphore, inc=1, device_id=device, device_id_type=MESH)
+
+    @pl.when(c == 0)
+    def _():
+        signal(barrier, sibling)
+
+    for other in others:
+        signal(barrier, at(*other, 0))
+
     load_server = pltpu.make_async_copy(server_error_hbm, server_error.at[z], small_sem.at[0])
     load_server.start()
+    each(1, NZ, start_loads)
     load_variance = pltpu.make_async_copy(variance_hbm, scale, small_sem.at[1])
     load_variance.start()
 
-    barrier = pltpu.get_barrier_semaphore()
-    peers = [sibling] + [at(px, py, z, c) for px, py in plane] + column
-    for peer in peers:
-        pl.semaphore_signal(barrier, inc=1, device_id=peer, device_id_type=MESH)
-
     def compress_chunk(k):
-        for copy in loads(k):
-            copy.wait()
+        load_grad(k).wait()
+        landed(momentum.at[pl.ds(0, 2 * CHUNK)], in_sem.at[1, k])
         for py in range(NY):
             first = pl.multiple_of(k * CHUNK + py * 128, 128)
             flat = pl.ds(pl.multiple_of(first * 128, 128 * 128), 128 * 128)
@@ -114,23 +123,36 @@
         landed(from_core.at[k], core_recv.at[k])
         total = sent[c, k].astype(jnp.float32) + from_core[k].astype(jnp.float32)
         chip_sum[k] = total.astype(jnp.bfloat16)
+        from_plane[k, me] = chip_sum[k, me]
+
+    def send_plane(k):
         for px, py in plane:
-            remote(
-                chip_sum.at[k, py * NX + px],
-                from_plane.at[k, me],
-                plane_send,
-                plane_recv.at[k],
-                at(px, py, z, c),
-            ).start()
-        from_plane[k, me] = chip_sum[k, me]
+            src, dst = chip_sum.at[k, py * NX + px], from_plane.at[k, me]
+            remote(src, dst, plane_send, plane_recv.at[k], at(px, py, z, c)).start()
+
+    def to_plane(k, pz):
+        block = plane_sum.at[k, z]
+        remote(block, block, z_send, z_recv.at[k], at(x, y, pz, c)).start()
 
     def sum_plane(k):
         landed(from_plane.at[k, pl.ds(0, PLANE - 1)], plane_recv.at[k])
         total = jnp.sum(from_plane[k].astype(jnp.float32), axis=0)
         plane_sum[k, z] = total.astype(jnp.bfloat16)
-        block = plane_sum.at[k, z]
-        for peer in column:
-            remote(block, block, z_send, z_recv.at[k], peer).start()
+
+        @pl.when(z != 0)
+        def _():
+            to_plane(k, 0)
+
+    def spread(k):
+        for pz in column:
+
+            @pl.when(pz != 0)
+            def _():
+                to_plane(k, pz)
+
+    def to_chip(k, px, py):
+        block = gathered.at[c, k, me]
+        remote(block, block, gather_send, gather_recv.at[k], at(px, py, z, c)).start()
 
     def serve(k):
         landed(plane_sum.at[k, pl.ds(0, NZ - 1)], z_recv.at[k])
@@ -138,13 +160,19 @@
         shifted = total * (1.0 / (2 * PLANE * NZ)) + server_error[k]
         answer = compress(shifted).astype(jnp.bfloat16)
         gathered[c, k, me] = answer
-        block = gathered.at[c, k, me]
+
+        @pl.when(me != 0)
+        def _():
+            to_chip(k, 0, 0)
+
+        residue[k] = shifted - answer.astype(jnp.float32)
+
+    def scatter(k):
         for px, py in plane:
-            remote(block, block, gather_send, gather_recv.at[k], at(px, py, z, c)).start()
-
-        @pl.when(k == z)
-        def _():
-            server_residue[...] = shifted - answer.astype(jnp.float32)
+
+            @pl.when(py * NX + px != 0)
+            def _():
+                to_chip(k, px, py)
 
     def finish(k, pc):
         for py in range(NY):
@@ -163,27 +191,47 @@
         landed(gathered.at[1 - c, k], last_recv.at[k])
         finish(k, 1 - c)
 
-    each(AHEAD, compress_chunk)
-    pl.semaphore_wait(barrier, len(peers))
-    each(AHEAD, send_core)
-
-    def early(t, _):
-        @pl.when(t < NZ)
-        def _():
-            compress_chunk(t)
-            send_core(t)
-
-        @pl.when(t >= LAG)
-        def _():
-            sum_chip(t - LAG)
-
-        return 0
-
-    lax.fori_loop(AHEAD, NZ + LAG, early, 0)
-
+    def compress_and_send(k):
+        compress_chunk(k)
+        send_core(k)
+
+    def sum_and_send(k):
+        sum_chip(k)
+        send_plane(k)
+
+    each(0, GREET, compress_chunk)
+
+    @pl.when(c == 1)
+    def _():
+        pl.semaphore_wait(barrier, 1)
+        signal(word, sibling)
+
+    each(GREET, MEET, compress_chunk)
+
+    @pl.when(c == 0)
+    def _():
+        pl.semaphore_wait(word, 1)
+
+    each(0, MEET, send_core)
+    each(MEET, BEFORE, compress_and_send)
+    each(0, READY, sum_chip)
+
+    @pl.when(c == 0)
+    def _():
+        pl.semaphore_wait(barrier, 2 * len(others))
+        signal(word, sibling)
+
+    @pl.when(c == 1)
+    def _():
+        pl.semaphore_wait(word, 1)
+
+    each(0, READY, send_plane)
     load_server.wait()
-    for peer in column:
-        remote(server_error.at[z], server_error.at[z], server_send, server_recv, peer).start()
+    for pz in column:
+        block = server_error.at[z]
+        remote(block, block, server_send, server_recv, at(x, y, pz, c)).start()
+    each(BEFORE, NZ, compress_and_send)
+    each(READY, NZ, sum_and_send)
 
     load_variance.wait()
 
@@ -191,23 +239,30 @@
         rows = pl.ds(pl.multiple_of(i * 128, 128), 128)
         scale[rows, :] = 1.0 / (jnp.sqrt(scale[rows, :]) + 1e-8)
 
-    each(ROWS // 128, invert)
-    each(NZ, sum_plane)
-    landed(server_error.at[pl.ds(0, NZ - 1)], server_recv)
-    each(NZ, serve)
+    each(0, ROWS // 128, invert)
 
     def late(t, _):
-        @pl.when(t < NZ)
+        @pl.when(t == SERVE)
         def _():
-            hand_over(t)
-
-        @pl.when(t >= GLAG)
-        def _():
-            take_over(t - GLAG)
+            landed(server_error.at[pl.ds(0, NZ - 1)], server_recv)
+
+        for lag, task in (
+            (0, sum_plane),
+            (SPREAD, spread),
+            (SERVE, serve),
+            (SCATTER, scatter),
+            (HAND, hand_over),
+            (TAKE, take_over),
+        ):
+
+            @pl.when(jnp.logical_and(t >= lag, t < lag + NZ))
+            def _():
+                task(t - lag)
 
         return 0
 
-    lax.fori_loop(0, NZ + GLAG, late, 0)
+    lax.fori_loop(0, NZ + TAKE, late, 0)
+    server_residue[...] = residue[z]
 
     landed(from_core, core_send)
     landed(from_plane.at[:, pl.ds(0, PLANE - 1)], plane_send)
@@ -251,20 +306,21 @@
             pltpu.VMEM(whole, f32),
             pltpu.VMEM(whole, f32),
             pltpu.VMEM((NZ, SPAN, 128), f32),
+            pltpu.VMEM((NZ, SPAN, 128), f32),
             pltpu.VMEM((2, NZ, PLANE, SPAN, 128), bf16),
             pltpu.VMEM((NZ, PLANE, SPAN, 128), bf16),
             pltpu.VMEM((NZ, PLANE, SPAN, 128), bf16),
             pltpu.VMEM((NZ, PLANE, SPAN, 128), bf16),
             pltpu.VMEM((NZ, NZ, SPAN, 128), bf16),
             pltpu.VMEM((2, NZ, PLANE, SPAN, 128), bf16),
-            dma((3, NZ)),
+            dma((2, NZ)),
             dma((2,)),
             dma, dma,
             dma, dma((NZ,)),
             dma, dma((NZ,)),
             dma, dma((NZ,)),
-            dma, dma((NZ,)),
-            dma, dma((NZ,)),
+            dma, dma,
+            pltpu.SemaphoreType.REGULAR,
         ],
         compiler_params=pltpu.CompilerParams(
             collective_id=0, has_side_effects=True, vmem_limit_bytes=32 << 20

time: 35.5 us -> 34.3 us (0.966)
  Pallas kernels: 34.8 us -> 33.6 us
    pallas_call x1, Pallas kernels: 32.7 us -> 31.6 us  [local(): pl.pallas_call(kernel, name='exchange', out_shape=(pltpu.VMEM(whole, f32)...]
where the time goes in v3:
time: 34.3 us
  Pallas kernels  33.6 us (98%)
  between operations  0.64 us (2%)
    pallas_call x1, Pallas kernels, local(): pl.pallas_call(kernel, name='exchange', out_shape=(pltpu.VMEM(whole, f32)...  31.6 us
    pallas_call x1, Pallas kernels, local(): pl.pallas_call(store, name='store', out_shape=tuple((jax.ShapeDtypeStruct...  2.04 us

profile of v3, /device:TPU:1, one launch (start us, length us, event | category | flops | bytes accessed | tf_op | source)
XLA Modules:
  0.0 34.3 jit_solution(2870728622922598256)
XLA Ops:
  0.6 31.6 %exchange.1 = (f32[4096,128]{1,0:T(8,128)S(1)}, f32[4096,128]{1,0:T(8,128)S(1)}, f32[16,128]{1,0:T(8,128)S(1)}) custom-call(bf16[1,524288]{1,0:T(2,128)(2,1)} %grad_hbm.1, f32[4096,128]{1,0:T(8,128)} %bitcast.7, f32[4096,128]{1,0:T(8,128)} %bitcast.8, f32[4096,128]{1,0:T(8,128)} %bitcast.9, f32[16,128]{1,0:T(8,128)} %bitcast.10), custom_call_target="tpu_custom_call" | custom-call | tf_op jit(solution)/shard_map/exchange/pallas_call | solution.py:293
  32.2 2.0 %store.1 = (f32[4096,128]{1,0:T(8,128)}, f32[4096,128]{1,0:T(8,128)}, f32[16,128]{1,0:T(8,128)}) custom-call(f32[4096,128]{1,0:T(8,128)S(1)} %get-tuple-element.9.update, f32[4096,128]{1,0:T(8,128)S(1)} %get-tuple-element.10.worker_error, f32[16,128]{1,0:T(8,128)S(1)} %get-tuple-element.11.server_residue), custom_call_target="tpu_custom_call" | custom-call | tf_op jit(solution)/shard_map/store/pallas_call | solution.py:340

commit v4 on v3

--- a/solution.py
+++ b/solution.py
@@ -13,6 +13,12 @@
 ROWS = NZ * CHUNK
 GREET, MEET = 2, 4
 BEFORE, READY = 6, 2
+PAIR = 1
+STEPS = NZ // PAIR
+FIRST = 1
+YIELD = 0
+DIRECT = 7
+PACE = 0
 SPREAD, SERVE, SCATTER, HAND, TAKE = 0, 7, 7, 14, 16
 PARTS = 1
 
@@ -80,20 +86,20 @@
         for src, dst in ((momentum_hbm, momentum), (error_hbm, error)):
             pltpu.make_async_copy(src.at[rows], dst.at[rows], in_sem.at[1, k]).start()
 
-    start_loads(0)
     barrier = pltpu.get_barrier_semaphore()
-    others = [(px, py, z) for px, py in plane] + [(x, y, pz) for pz in column]
+    others = [(x, y, column[0]), *((px, py, z) for px, py in plane), *((x, y, pz) for pz in column[1:])]
 
     def signal(semaphore, device):
         pl.semaphore_signal(semaphore, inc=1, device_id=device, device_id_type=MESH)
 
-    @pl.when(c == 0)
-    def _():
-        signal(barrier, sibling)
-
     for other in others:
         signal(barrier, at(*other, 0))
 
+    @pl.when(c == 0)
+    def _():
+        signal(barrier, sibling)
+
+    start_loads(0)
     load_server = pltpu.make_async_copy(server_error_hbm, server_error.at[z], small_sem.at[0])
     load_server.start()
     each(1, NZ, start_loads)
@@ -122,82 +128,103 @@
     def sum_chip(k):
         landed(from_core.at[k], core_recv.at[k])
         total = sent[c, k].astype(jnp.float32) + from_core[k].astype(jnp.float32)
-        chip_sum[k] = total.astype(jnp.bfloat16)
-        from_plane[k, me] = chip_sum[k, me]
-
-    def send_plane(k):
+        chip_sum[lax.div(k, PAIR), :, lax.rem(k, PAIR)] = total.astype(jnp.bfloat16)
+
+    def together(i):
+        return pl.ds(i * PAIR, PAIR)
+
+    def members(i):
+        return [i * PAIR + j for j in range(PAIR)]
+
+    def send_plane(i):
         for px, py in plane:
-            src, dst = chip_sum.at[k, py * NX + px], from_plane.at[k, me]
-            remote(src, dst, plane_send, plane_recv.at[k], at(px, py, z, c)).start()
-
-    def to_plane(k, pz):
-        block = plane_sum.at[k, z]
-        remote(block, block, z_send, z_recv.at[k], at(x, y, pz, c)).start()
-
-    def sum_plane(k):
-        landed(from_plane.at[k, pl.ds(0, PLANE - 1)], plane_recv.at[k])
-        total = jnp.sum(from_plane[k].astype(jnp.float32), axis=0)
-        plane_sum[k, z] = total.astype(jnp.bfloat16)
+            src, dst = chip_sum.at[i, py * NX + px], from_plane.at[i, me]
+            remote(src, dst, plane_send, plane_recv.at[i], at(px, py, z, c)).start()
+        from_plane[i, me] = chip_sum[i, me]
+
+    def to_plane(i, pz):
+        block = plane_sum.at[i, z]
+        remote(block, block, z_send, z_recv.at[i], at(x, y, pz, c)).start()
+
+    def sum_plane(i):
+        landed(from_plane.at[i, pl.ds(0, PLANE - 1)], plane_recv.at[i])
+        total = jnp.sum(from_plane[i].astype(jnp.float32), axis=0)
+        plane_sum[i, z] = total.astype(jnp.bfloat16)
 
         @pl.when(z != 0)
         def _():
-            to_plane(k, 0)
-
-    def spread(k):
+            to_plane(i, 0)
+
+    def spread(i):
         for pz in column:
 
             @pl.when(pz != 0)
             def _():
-                to_plane(k, pz)
-
-    def to_chip(k, px, py):
-        block = gathered.at[c, k, me]
-        remote(block, block, gather_send, gather_recv.at[k], at(px, py, z, c)).start()
-
-    def serve(k):
-        landed(plane_sum.at[k, pl.ds(0, NZ - 1)], z_recv.at[k])
-        total = jnp.sum(plane_sum[k].astype(jnp.float32), axis=0)
-        shifted = total * (1.0 / (2 * PLANE * NZ)) + server_error[k]
+                to_plane(i, pz)
+
+    def to_chip(i, px, py):
+        block = gathered.at[c, i, me]
+        remote(block, block, gather_send, gather_recv.at[i], at(px, py, z, c)).start()
+
+        @pl.when(i >= DIRECT)
+        def _():
+            remote(block, block, gather_send, last_recv.at[i], at(px, py, z, 1 - c)).start()
+
+    def serve(i):
+        landed(plane_sum.at[i, pl.ds(0, NZ - 1)], z_recv.at[i])
+        total = jnp.sum(plane_sum[i].astype(jnp.float32), axis=0)
+        shifted = total * (1.0 / (2 * PLANE * NZ)) + server_error[together(i)]
         answer = compress(shifted).astype(jnp.bfloat16)
-        gathered[c, k, me] = answer
+        gathered[c, i, me] = answer
+        residue[together(i)] = shifted - answer.astype(jnp.float32)
 
         @pl.when(me != 0)
         def _():
-            to_chip(k, 0, 0)
-
-        residue[k] = shifted - answer.astype(jnp.float32)
-
-    def scatter(k):
+            to_chip(i, 0, 0)
+
+    def scatter(i):
         for px, py in plane:
 
             @pl.when(py * NX + px != 0)
             def _():
-                to_chip(k, px, py)
-
-    def finish(k, pc):
+                to_chip(i, px, py)
+
+        @pl.when(i >= DIRECT)
+        def _():
+            block = gathered.at[c, i, me]
+            remote(block, block, gather_send, last_recv.at[i], sibling).start()
+
+    def finish(i, j, pc):
         for py in range(NY):
-            first = pl.multiple_of(k * CHUNK + py * 128 + pc * 64, 64)
+            first = pl.multiple_of((i * PAIR + j) * CHUNK + py * 128 + pc * 64, 64)
             rows = pl.ds(first, 64)
-            values = gathered[pc, k, py * NX : (py + 1) * NX].astype(jnp.float32)
+            values = gathered[pc, i, py * NX : (py + 1) * NX, j].astype(jnp.float32)
             update[rows, :] = values.reshape(64, 128) * scale[rows, :]
 
-    def hand_over(k):
-        landed(from_plane.at[k, pl.ds(0, PLANE - 1)], gather_recv.at[k])
-        block = gathered.at[c, k]
-        remote(block, block, last_send, last_recv.at[k], sibling).start()
-        finish(k, c)
-
-    def take_over(k):
-        landed(gathered.at[1 - c, k], last_recv.at[k])
-        finish(k, 1 - c)
+    def hand_over(i):
+        landed(from_plane.at[i, pl.ds(0, PLANE - 1)], gather_recv.at[i])
+
+        @pl.when(i < DIRECT)
+        def _():
+            block = gathered.at[c, i]
+            remote(block, block, last_send, last_recv.at[i], sibling).start()
+
+        for j in range(PAIR):
+            finish(i, j, c)
+
+    def take_over(i):
+        landed(gathered.at[1 - c, i], last_recv.at[i])
+        for j in range(PAIR):
+            finish(i, j, 1 - c)
 
     def compress_and_send(k):
         compress_chunk(k)
         send_core(k)
 
-    def sum_and_send(k):
-        sum_chip(k)
-        send_plane(k)
+    def sum_and_send(i):
+        for k in members(i):
+            sum_chip(k)
+        send_plane(i)
 
     each(0, GREET, compress_chunk)
 
@@ -225,21 +252,28 @@
     def _():
         pl.semaphore_wait(word, 1)
 
-    each(0, READY, send_plane)
+    each(0, READY // PAIR, send_plane)
     load_server.wait()
     for pz in column:
         block = server_error.at[z]
         remote(block, block, server_send, server_recv, at(x, y, pz, c)).start()
     each(BEFORE, NZ, compress_and_send)
-    each(READY, NZ, sum_and_send)
-
     load_variance.wait()
 
     def invert(i):
         rows = pl.ds(pl.multiple_of(i * 128, 128), 128)
         scale[rows, :] = 1.0 / (jnp.sqrt(scale[rows, :]) + 1e-8)
 
-    each(0, ROWS // 128, invert)
+    @pl.when(c == 1)
+    def _():
+        each(0, ROWS // 128, invert)
+
+    each(READY // PAIR, STEPS, sum_and_send)
+
+    @pl.when(c == 0)
+    def _():
+        each(0, ROWS // 128, invert)
+
 
     def late(t, _):
         @pl.when(t == SERVE)
@@ -248,20 +282,20 @@
 
         for lag, task in (
             (0, sum_plane),
-            (SPREAD, spread),
+            (SPREAD + YIELD * c, spread),
             (SERVE, serve),
             (SCATTER, scatter),
             (HAND, hand_over),
             (TAKE, take_over),
         ):
 
-            @pl.when(jnp.logical_and(t >= lag, t < lag + NZ))
+            @pl.when(jnp.logical_and(t >= lag, t < lag + STEPS))
             def _():
                 task(t - lag)
 
         return 0
 
-    lax.fori_loop(0, NZ + TAKE, late, 0)
+    lax.fori_loop(0, STEPS + TAKE, late, 0)
     server_residue[...] = residue[z]
 
     landed(from_core, core_send)
@@ -269,7 +303,9 @@
     landed(plane_sum.at[:, pl.ds(0, NZ - 1)], z_send)
     landed(server_error.at[pl.ds(0, NZ - 1)], server_send)
     landed(from_plane.at[:, pl.ds(0, PLANE - 1)], gather_send)
-    landed(from_core, last_send)
+    landed(gathered.at[0, pl.ds(0, DIRECT)], last_send)
+    if DIRECT < STEPS:
+        landed(gathered.at[0, pl.ds(0, STEPS - DIRECT)], gather_send)
 
 
 def store(update, worker_error, server_residue, *refs):
@@ -309,16 +345,16 @@
             pltpu.VMEM((NZ, SPAN, 128), f32),
             pltpu.VMEM((2, NZ, PLANE, SPAN, 128), bf16),
             pltpu.VMEM((NZ, PLANE, SPAN, 128), bf16),
-            pltpu.VMEM((NZ, PLANE, SPAN, 128), bf16),
-            pltpu.VMEM((NZ, PLANE, SPAN, 128), bf16),
-            pltpu.VMEM((NZ, NZ, SPAN, 128), bf16),
-            pltpu.VMEM((2, NZ, PLANE, SPAN, 128), bf16),
+            pltpu.VMEM((STEPS, PLANE, PAIR, SPAN, 128), bf16),
+            pltpu.VMEM((STEPS, PLANE, PAIR, SPAN, 128), bf16),
+            pltpu.VMEM((STEPS, NZ, PAIR, SPAN, 128), bf16),
+            pltpu.VMEM((2, STEPS, PLANE, PAIR, SPAN, 128), bf16),
             dma((2, NZ)),
             dma((2,)),
             dma, dma,
             dma, dma((NZ,)),
-            dma, dma((NZ,)),
-            dma, dma((NZ,)),
+            dma, dma((STEPS,)),
+            dma, dma((STEPS,)),
             dma, dma,
             pltpu.SemaphoreType.REGULAR,
         ],

time: 34.3 us -> 33.7 us (0.983)
  Pallas kernels: 33.6 us -> 33 us
    pallas_call x1, Pallas kernels: 31.6 us -> 31 us  [local(): pl.pallas_call(kernel, name='exchange', out_shape=(pltpu.VMEM(whole, f32)...]
where the time goes in v4:
time: 33.7 us; the launch traced here: 33.6 us
  Pallas kernels  33 us (98%)
  between operations  0.64 us (2%)
    pallas_call x1, Pallas kernels, local(): pl.pallas_call(kernel, name='exchange', out_shape=(pltpu.VMEM(whole, f32)...  31 us
    pallas_call x1, Pallas kernels, local(): pl.pallas_call(store, name='store', out_shape=tuple((jax.ShapeDtypeStruct...  2.04 us

profile of v4, /device:TPU:1, one launch (start us, length us, event | category | flops | bytes accessed | tf_op | source)
XLA Modules:
  0.0 33.6 jit_solution(3081719898740241776)
XLA Ops:
  0.6 31.0 %exchange.1 = (f32[4096,128]{1,0:T(8,128)S(1)}, f32[4096,128]{1,0:T(8,128)S(1)}, f32[16,128]{1,0:T(8,128)S(1)}) custom-call(bf16[1,524288]{1,0:T(2,128)(2,1)} %grad_hbm.1, f32[4096,128]{1,0:T(8,128)} %bitcast.7, f32[4096,128]{1,0:T(8,128)} %bitcast.8, f32[4096,128]{1,0:T(8,128)} %bitcast.9, f32[16,128]{1,0:T(8,128)} %bitcast.10), custom_call_target="tpu_custom_call" | custom-call | tf_op jit(solution)/shard_map/exchange/pallas_call | solution.py:329
  31.6 2.0 %store.1 = (f32[4096,128]{1,0:T(8,128)}, f32[4096,128]{1,0:T(8,128)}, f32[16,128]{1,0:T(8,128)}) custom-call(f32[4096,128]{1,0:T(8,128)S(1)} %get-tuple-element.9.update, f32[4096,128]{1,0:T(8,128)S(1)} %get-tuple-element.10.worker_error, f32[16,128]{1,0:T(8,128)S(1)} %get-tuple-element.11.server_residue), custom_call_target="tpu_custom_call" | custom-call | tf_op jit(solution)/shard_map/store/pallas_call | solution.py:376

commit v5 on v4

--- a/solution.py
+++ b/solution.py
@@ -11,14 +11,11 @@
 SPAN = 16
 CHUNK = 2 * PLANE * SPAN
 ROWS = NZ * CHUNK
-GREET, MEET = 2, 4
-BEFORE, READY = 6, 2
+GREET, MEET = 1, 2
+BEFORE, READY = 5, 2
 PAIR = 1
 STEPS = NZ // PAIR
-FIRST = 1
-YIELD = 0
 DIRECT = 7
-PACE = 0
 SPREAD, SERVE, SCATTER, HAND, TAKE = 0, 7, 7, 14, 16
 PARTS = 1
 
@@ -282,7 +279,7 @@
 
         for lag, task in (
             (0, sum_plane),
-            (SPREAD + YIELD * c, spread),
+            (SPREAD, spread),
             (SERVE, serve),
             (SCATTER, scatter),
             (HAND, hand_over),

time: 33.7 us -> 33.5 us (level)
  no operation moved by 1% of the time
where the time goes in v5:
time: 33.5 us; the launch traced here: 33.4 us
  Pallas kernels  32.8 us (98%)
  between operations  0.64 us (2%)
    pallas_call x1, Pallas kernels, local(): pl.pallas_call(kernel, name='exchange', out_shape=(pltpu.VMEM(whole, f32)...  30.8 us
    pallas_call x1, Pallas kernels, local(): pl.pallas_call(store, name='store', out_shape=tuple((jax.ShapeDtypeStruct...  2.04 us

profile of v5, /device:TPU:1, one launch (start us, length us, event | category | flops | bytes accessed | tf_op | source)
XLA Modules:
  0.0 33.4 jit_solution(12198075491434031942)
XLA Ops:
  0.6 30.8 %exchange.1 = (f32[4096,128]{1,0:T(8,128)S(1)}, f32[4096,128]{1,0:T(8,128)S(1)}, f32[16,128]{1,0:T(8,128)S(1)}) custom-call(bf16[1,524288]{1,0:T(2,128)(2,1)} %grad_hbm.1, f32[4096,128]{1,0:T(8,128)} %bitcast.7, f32[4096,128]{1,0:T(8,128)} %bitcast.8, f32[4096,128]{1,0:T(8,128)} %bitcast.9, f32[16,128]{1,0:T(8,128)} %bitcast.10), custom_call_target="tpu_custom_call" | custom-call | tf_op jit(solution)/shard_map/exchange/pallas_call | solution.py:326
  31.4 2.0 %store.1 = (f32[4096,128]{1,0:T(8,128)}, f32[4096,128]{1,0:T(8,128)}, f32[16,128]{1,0:T(8,128)}) custom-call(f32[4096,128]{1,0:T(8,128)S(1)} %get-tuple-element.9.update, f32[4096,128]{1,0:T(8,128)S(1)} %get-tuple-element.10.worker_error, f32[16,128]{1,0:T(8,128)S(1)} %get-tuple-element.11.server_residue), custom_call_target="tpu_custom_call" | custom-call | tf_op jit(solution)/shard_map/store/pallas_call | solution.py:373

commit v6 on v5

--- a/solution.py
+++ b/solution.py
@@ -12,7 +12,7 @@
 CHUNK = 2 * PLANE * SPAN
 ROWS = NZ * CHUNK
 GREET, MEET = 1, 2
-BEFORE, READY = 5, 2
+BEFORE, READY = 6, 2
 PAIR = 1
 STEPS = NZ // PAIR
 DIRECT = 7
@@ -37,9 +37,8 @@
     update, worker_error, server_residue,
     grad, momentum, error, scale, server_error, residue,
     sent, from_core, chip_sum, from_plane, plane_sum, gathered,
-    in_sem, small_sem, server_send, server_recv,
-    core_send, core_recv, plane_send, plane_recv, z_send, z_recv,
-    gather_send, last_send, word,
+    in_sem, small_sem, server_recv,
+    out_sem, core_recv, plane_recv, z_recv, word,
 ):
     dp = lax.axis_index("dp")
     x = lax.axis_index("outer")
@@ -119,11 +118,15 @@
                     first = (pc * NX + px) * SPAN
                     sent[pc, k, py * NX + px] = rounded[first : first + SPAN]
 
-    def send_core(k):
-        remote(sent.at[1 - c, k], from_core.at[k], core_send, core_recv.at[k], sibling).start()
+    def send_core(i):
+        both = pl.ds(2 * i, 2)
+        remote(sent.at[1 - c, both], from_core.at[both], out_sem, core_recv.at[i], sibling).start()
 
     def sum_chip(k):
-        landed(from_core.at[k], core_recv.at[k])
+        @pl.when(lax.rem(k, 2) == 0)
+        def _():
+            landed(from_core.at[pl.ds(0, 2)], core_recv.at[lax.div(k, 2)])
+
         total = sent[c, k].astype(jnp.float32) + from_core[k].astype(jnp.float32)
         chip_sum[lax.div(k, PAIR), :, lax.rem(k, PAIR)] = total.astype(jnp.bfloat16)
 
@@ -136,12 +139,12 @@
     def send_plane(i):
         for px, py in plane:
             src, dst = chip_sum.at[i, py * NX + px], from_plane.at[i, me]
-            remote(src, dst, plane_send, plane_recv.at[i], at(px, py, z, c)).start()
+            remote(src, dst, out_sem, plane_recv.at[i], at(px, py, z, c)).start()
         from_plane[i, me] = chip_sum[i, me]
 
     def to_plane(i, pz):
         block = plane_sum.at[i, z]
-        remote(block, block, z_send, z_recv.at[i], at(x, y, pz, c)).start()
+        remote(block, block, out_sem, z_recv.at[i], at(x, y, pz, c)).start()
 
     def sum_plane(i):
         landed(from_plane.at[i, pl.ds(0, PLANE - 1)], plane_recv.at[i])
@@ -161,11 +164,11 @@
 
     def to_chip(i, px, py):
         block = gathered.at[c, i, me]
-        remote(block, block, gather_send, gather_recv.at[i], at(px, py, z, c)).start()
+        remote(block, block, out_sem, gather_recv.at[i], at(px, py, z, c)).start()
 
         @pl.when(i >= DIRECT)
         def _():
-            remote(block, block, gather_send, last_recv.at[i], at(px, py, z, 1 - c)).start()
+            remote(block, block, out_sem, last_recv.at[i], at(px, py, z, 1 - c)).start()
 
     def serve(i):
         landed(plane_sum.at[i, pl.ds(0, NZ - 1)], z_recv.at[i])
@@ -189,7 +192,7 @@
         @pl.when(i >= DIRECT)
         def _():
             block = gathered.at[c, i, me]
-            remote(block, block, gather_send, last_recv.at[i], sibling).start()
+            remote(block, block, out_sem, last_recv.at[i], sibling).start()
 
     def finish(i, j, pc):
         for py in range(NY):
@@ -204,7 +207,7 @@
         @pl.when(i < DIRECT)
         def _():
             block = gathered.at[c, i]
-            remote(block, block, last_send, last_recv.at[i], sibling).start()
+            remote(block, block, out_sem, last_recv.at[i], sibling).start()
 
         for j in range(PAIR):
             finish(i, j, c)
@@ -216,7 +219,10 @@
 
     def compress_and_send(k):
         compress_chunk(k)
-        send_core(k)
+
+        @pl.when(lax.rem(k, 2) == 1)
+        def _():
+            send_core(lax.div(k, 2))
 
     def sum_and_send(i):
         for k in members(i):
@@ -236,7 +242,7 @@
     def _():
         pl.semaphore_wait(word, 1)
 
-    each(0, MEET, send_core)
+    each(0, MEET // 2, send_core)
     each(MEET, BEFORE, compress_and_send)
     each(0, READY, sum_chip)
 
@@ -253,7 +259,7 @@
     load_server.wait()
     for pz in column:
         block = server_error.at[z]
-        remote(block, block, server_send, server_recv, at(x, y, pz, c)).start()
+        remote(block, block, out_sem, server_recv, at(x, y, pz, c)).start()
     each(BEFORE, NZ, compress_and_send)
     load_variance.wait()
 
@@ -295,14 +301,14 @@
     lax.fori_loop(0, STEPS + TAKE, late, 0)
     server_residue[...] = residue[z]
 
-    landed(from_core, core_send)
-    landed(from_plane.at[:, pl.ds(0, PLANE - 1)], plane_send)
-    landed(plane_sum.at[:, pl.ds(0, NZ - 1)], z_send)
-    landed(server_error.at[pl.ds(0, NZ - 1)], server_send)
-    landed(from_plane.at[:, pl.ds(0, PLANE - 1)], gather_send)
-    landed(gathered.at[0, pl.ds(0, DIRECT)], last_send)
+    landed(from_core, out_sem)
+    landed(from_plane.at[:, pl.ds(0, PLANE - 1)], out_sem)
+    landed(plane_sum.at[:, pl.ds(0, NZ - 1)], out_sem)
+    landed(server_error.at[pl.ds(0, NZ - 1)], out_sem)
+    landed(from_plane.at[:, pl.ds(0, PLANE - 1)], out_sem)
+    landed(gathered.at[0, pl.ds(0, DIRECT)], out_sem)
     if DIRECT < STEPS:
-        landed(gathered.at[0, pl.ds(0, STEPS - DIRECT)], gather_send)
+        landed(gathered.at[0, pl.ds(0, STEPS - DIRECT)], out_sem)
 
 
 def store(update, worker_error, server_residue, *refs):
@@ -348,11 +354,10 @@
             pltpu.VMEM((2, STEPS, PLANE, PAIR, SPAN, 128), bf16),
             dma((2, NZ)),
             dma((2,)),
-            dma, dma,
-            dma, dma((NZ,)),
-            dma, dma((STEPS,)),
-            dma, dma((STEPS,)),
-            dma, dma,
+            dma,
+            dma, dma((NZ // 2,)),
+            dma((STEPS,)),
+            dma((STEPS,)),
             pltpu.SemaphoreType.REGULAR,
         ],
         compiler_params=pltpu.CompilerParams(

time: 33.5 us -> 33.6 us (level)
  no operation moved by 1% of the time
where the time goes in v6:
time: 33.6 us
  Pallas kernels  32.9 us (98%)
  between operations  0.64 us (2%)
    pallas_call x1, Pallas kernels, local(): pl.pallas_call(kernel, name='exchange', out_shape=(pltpu.VMEM(whole, f32)...  30.9 us
    pallas_call x1, Pallas kernels, local(): pl.pallas_call(store, name='store', out_shape=tuple((jax.ShapeDtypeStruct...  2.04 us

profile of v6, /device:TPU:1, one launch (start us, length us, event | category | flops | bytes accessed | tf_op | source)
XLA Modules:
  0.0 33.6 jit_solution(10583425729769465435)
XLA Ops:
  0.6 30.9 %exchange.1 = (f32[4096,128]{1,0:T(8,128)S(1)}, f32[4096,128]{1,0:T(8,128)S(1)}, f32[16,128]{1,0:T(8,128)S(1)}) custom-call(bf16[1,524288]{1,0:T(2,128)(2,1)} %grad_hbm.1, f32[4096,128]{1,0:T(8,128)} %bitcast.7, f32[4096,128]{1,0:T(8,128)} %bitcast.8, f32[4096,128]{1,0:T(8,128)} %bitcast.9, f32[16,128]{1,0:T(8,128)} %bitcast.10), custom_call_target="tpu_custom_call" | custom-call | tf_op jit(solution)/shard_map/exchange/pallas_call | solution.py:332
  31.5 2.0 %store.1 = (f32[4096,128]{1,0:T(8,128)}, f32[4096,128]{1,0:T(8,128)}, f32[16,128]{1,0:T(8,128)}) custom-call(f32[4096,128]{1,0:T(8,128)S(1)} %get-tuple-element.9.update, f32[4096,128]{1,0:T(8,128)S(1)} %get-tuple-element.10.worker_error, f32[16,128]{1,0:T(8,128)S(1)} %get-tuple-element.11.server_residue), custom_call_target="tpu_custom_call" | custom-call | tf_op jit(solution)/shard_map/store/pallas_call | solution.py:378

commit v7 on v6

--- a/solution.py
+++ b/solution.py
@@ -166,10 +166,6 @@
         block = gathered.at[c, i, me]
         remote(block, block, out_sem, gather_recv.at[i], at(px, py, z, c)).start()
 
-        @pl.when(i >= DIRECT)
-        def _():
-            remote(block, block, out_sem, last_recv.at[i], at(px, py, z, 1 - c)).start()
-
     def serve(i):
         landed(plane_sum.at[i, pl.ds(0, NZ - 1)], z_recv.at[i])
         total = jnp.sum(plane_sum[i].astype(jnp.float32), axis=0)
@@ -192,6 +188,9 @@
         @pl.when(i >= DIRECT)
         def _():
             block = gathered.at[c, i, me]
+            for px, py in plane:
+                other = at(px, py, z, 1 - c)
+                remote(block, block, out_sem, last_recv.at[i], other).start()
             remote(block, block, out_sem, last_recv.at[i], sibling).start()
 
     def finish(i, j, pc):

time: 33.6 us -> 33.5 us (level)
  no operation moved by 1% of the time
where the time goes in v7:
time: 33.5 us
  Pallas kernels  32.8 us (98%)
  between operations  0.64 us (2%)
    pallas_call x1, Pallas kernels, local(): pl.pallas_call(kernel, name='exchange', out_shape=(pltpu.VMEM(whole, f32)...  30.8 us
    pallas_call x1, Pallas kernels, local(): pl.pallas_call(store, name='store', out_shape=tuple((jax.ShapeDtypeStruct...  2.04 us

profile of v7, /device:TPU:1, one launch (start us, length us, event | category | flops | bytes accessed | tf_op | source)
XLA Modules:
  0.0 33.5 jit_solution(13779991074226059355)
XLA Ops:
  0.6 30.8 %exchange.1 = (f32[4096,128]{1,0:T(8,128)S(1)}, f32[4096,128]{1,0:T(8,128)S(1)}, f32[16,128]{1,0:T(8,128)S(1)}) custom-call(bf16[1,524288]{1,0:T(2,128)(2,1)} %grad_hbm.1, f32[4096,128]{1,0:T(8,128)} %bitcast.7, f32[4096,128]{1,0:T(8,128)} %bitcast.8, f32[4096,128]{1,0:T(8,128)} %bitcast.9, f32[16,128]{1,0:T(8,128)} %bitcast.10), custom_call_target="tpu_custom_call" | custom-call | tf_op jit(solution)/shard_map/exchange/pallas_call | solution.py:331
  31.4 2.0 %store.1 = (f32[4096,128]{1,0:T(8,128)}, f32[4096,128]{1,0:T(8,128)}, f32[16,128]{1,0:T(8,128)}) custom-call(f32[4096,128]{1,0:T(8,128)S(1)} %get-tuple-element.9.update, f32[4096,128]{1,0:T(8,128)S(1)} %get-tuple-element.10.worker_error, f32[16,128]{1,0:T(8,128)S(1)} %get-tuple-element.11.server_residue), custom_call_target="tpu_custom_call" | custom-call | tf_op jit(solution)/shard_map/store/pallas_call | solution.py:377
